TPU v7x, 32 devices: a whole 2x2x4 slice. The times are simulated.
32 devices in a mesh: dp: 2 (over y), expert: 16 (over z, x, core).
Axes of the slice: x: 2, y: 2, z: 4, core: 2. Of those that a mesh axis runs over, the one named last changes fastest.
Arguments:
- cache: bfloat16 [4, 64, 1152], P('dp'), may hold values from -6 to 6
- requests: int32 [2, 16, 2], P(None, 'expert'), may hold values from 0 to 3
- routes: int32 [4096, 1], P('expert'), may hold values from 0 to 15; in each aligned block of 256 rows (0 to 255, 256 to 511, ...) at most 20 rows name the same one
- combine_weight: float32 [4096, 1], P('expert'), may hold values from 0.2 to 1
- proj_weight: bfloat16 [1152, 2048], P('expert', 'dp'), may hold values from -1 to 1
- norm_gain: float32 [2048], replicated, may hold values from 0.5 to 1.5
- gate_weight: bfloat16 [16, 2048, 1408], P('expert', None, 'dp'), may hold values from -0.125 to 0.125
- up_weight: bfloat16 [16, 2048, 1408], P('expert', None, 'dp'), may hold values from -0.125 to 0.125
- down_weight: bfloat16 [16, 1408, 2048], P('expert', None, 'dp'), may hold values from -0.15625 to 0.15625
- cotangent: bfloat16 [4096, 2048], P('expert', 'dp'), may hold values from -6 to 6
Outputs:
- mixed: bfloat16 [4096, 2048], P('expert', 'dp')
- down_grad: bfloat16 [16, 1408, 2048], P('expert', None, 'dp')
Inputs may be any that keep to these rules, and one draw needn't show every extreme that they name: `routes`: among the 256 tokens of one column no expert is named more than 20 times, and in every draw some column names some expert exactly 20 times.
All inputs are finite; a program needn't handle non-finite values.
Results may differ from a plain program's by a relative error of at most 0.012.
Values may be sent and summed in bfloat16 or wider, within the bound.
A program may use at most 64 MiB of HBM per device.

v0:
```python
import jax
import jax.numpy as jnp
from jax import lax
from jax.sharding import PartitionSpec as P

BF = jnp.bfloat16
F32 = jnp.float32


def dot(a, b, dims=((1,), (0,))):
    return lax.dot_general(a, b, (dims, ((), ())), preferred_element_type=F32)


def body(
    cache,
    requests,
    routes,
    combine_weight,
    proj_weight,
    norm_gain,
    gate_weight,
    up_weight,
    down_weight,
    cotangent,
):
    width = cotangent.shape[1]
    n_expert = lax.axis_size("expert")
    experts = n_expert * gate_weight.shape[0]
    block, feat = cache.shape[1:]
    feats = lax.all_gather(cache, "dp", axis=0, tiled=True).reshape(-1, feat)
    lanes = width // n_expert
    piece = lax.all_to_all(
        proj_weight.reshape(-1, n_expert, lanes), "expert", split_axis=1, concat_axis=0, tiled=True
    ).reshape(feat, lanes)
    part = dot(feats, piece).astype(BF)
    projected = lax.all_gather(part, ("dp", "expert"), axis=1, tiled=True)
    values = projected.astype(F32)
    mean_square = jnp.mean(values * values, axis=1)
    table = (values * lax.rsqrt(mean_square + 1e-06)[:, None] * norm_gain[None, :]).astype(BF)
    table_rows = table.shape[0]
    token_row = (
        requests.reshape(-1)[:, None] * block + jnp.arange(block, dtype=jnp.int32)[None, :]
    ).reshape(-1)
    tokens = token_row.shape[0]
    capacity = max(2, 5 * tokens // (4 * experts))
    expert_id = routes[:, 0]
    order = jnp.arange(tokens, dtype=jnp.int32)
    earlier = (expert_id[:, None] == expert_id[None, :]) & (order[None, :] < order[:, None])
    slot_rank = jnp.sum(earlier.astype(jnp.int32), axis=1)
    position = expert_id * capacity + slot_rank
    hit = jnp.arange(experts * capacity, dtype=jnp.int32)[:, None] == position[None, :]
    pick = hit.astype(BF)
    slot_row = jnp.sum(jnp.where(hit, token_row[None, :] + 1, 0), axis=1) - 1
    token_weight = combine_weight[:, 0]
    scaled_grad = (token_weight[:, None] * cotangent.astype(F32)).astype(BF)
    sent = dot(pick, scaled_grad).astype(BF).reshape(experts, capacity, width)
    grad_rows = lax.all_to_all(sent, "expert", split_axis=0, concat_axis=0, tiled=True)
    grad_rows = grad_rows.reshape(-1, width)
    rows = lax.all_to_all(
        slot_row.reshape(experts, capacity), "expert", split_axis=0, concat_axis=0, tiled=True
    ).reshape(-1)
    select = (rows[:, None] == jnp.arange(table_rows, dtype=jnp.int32)[None, :]).astype(BF)
    gate_act = dot(table, gate_weight[0])
    up_act = dot(table, up_weight[0])
    half = (jax.nn.silu(gate_act) * up_act).astype(BF)
    hidden = lax.all_gather(half, "dp", axis=1, tiled=True)
    out_rows = dot(hidden, down_weight[0]).astype(BF)
    sent_out = dot(select, out_rows).astype(BF).reshape(-1, capacity, width)
    hidden_rows = dot(select, hidden).astype(BF)
    down_grad = dot(hidden_rows, grad_rows, ((0,), (0,))).astype(BF)
    returned = lax.all_to_all(sent_out, "expert", split_axis=0, concat_axis=0, tiled=True)
    token_out = dot(pick, returned.reshape(experts * capacity, width), ((0,), (0,)))
    mixed = (token_weight[:, None] * token_out).astype(BF)
    return (mixed, down_grad[None])


def solution(mesh):
    return jax.shard_map(
        body,
        mesh=mesh,
        in_specs=(
            P("dp", None, None),
            P(None, "expert", None),
            P("expert", None),
            P("expert", None),
            P("expert", "dp"),
            P(),
            P("expert", None, "dp"),
            P("expert", None, "dp"),
            P("expert", None, "dp"),
            P("expert", "dp"),
        ),
        out_specs=(P("expert", "dp"), P("expert", None, "dp")),
        check_vma=False,
    )
```

profile of v0, /device:TPU:9, one launch (start us, length us, event | category | flops | bytes accessed | tf_op | source)
XLA Modules:
  0.0 144.0 jit_solution(15097482984221297119)
XLA Ops:
  7.2 0.0 copy-start
  7.2 0.0 copy-start.4
  7.2 0.0 copy-start.2
  7.2 0.0 copy-start.3
  7.2 1.9 %copy.17 = bf16[72,1024]{0,1:T(8,128)(2,1)} copy(bf16[72,1024]{1,0:T(8,128)(2,1)} %param.14) | data formatting | bytes 294912 | tf_op jit(solution)/shard_map/reshape | solution.py:33
  9.1 6.6 %all-to-all-start.1 = ((bf16[72,16,64]{0,2,1:T(8,128)(2,1)}), bf16[72,16,64]{0,2,1:T(8,128)(2,1)}, u32[]{:S(2)}, u32[]{:S(2)}) async-start(bf16[72,16,64]{0,2,1:T(8,128)(2,1)} %bitcast.3), calls=%async_computation.1 | async-start | bytes 524288 | tf_op jit(solution)/shard_map/all_to_all | solution.py:32
  15.7 0.0 all-gather.2.cloned.1.call-start
  15.7 9.1 %all_gather.9 = bf16[4,64,1152]{2,1,0:T(8,128)(2,1)S(1)} all-gather(bf16[2,64,1152]{2,1,0:T(8,128)(2,1)} %param.10), channel_id=1, replica_groups=mesh['dp'=2,'expert'=16] {'dp'}, dimensions={0}, use_global_device_ids=true | all-gather | bytes 884736 | tf_op jit(solution)/shard_map/all_gather | solution.py:30
  24.9 0.0 all-to-all-done.1
  24.9 1.8 %copy.16 = bf16[16,72,1,64]{1,0,3,2:T(8,128)(2,1)} copy(bf16[16,72,1,64]{1,3,0,2:T(8,128)(2,1)} %bitcast.5) | data formatting | bytes 294912 | tf_op jit(solution)/shard_map/all_to_all | solution.py:32
  26.7 1.9 %reshape.87 = bf16[1152,64]{0,1:T(8,128)(2,1)} reshape(bf16[16,72,1,64]{1,0,3,2:T(8,128)(2,1)} %copy.16) | data formatting | bytes 294912 | tf_op jit(solution)/shard_map/reshape | solution.py:34
  28.6 1.8 %convolution_convert_fusion.4 = bf16[256,64]{0,1:T(8,128)(2,1)} fusion(bf16[256,1152]{1,0:T(8,128)(2,1)S(1)} %bitcast.36, bf16[1152,64]{0,1:T(8,128)(2,1)} %reshape.87), kind=kOutput, calls=%fused_computation.21 | convolution fusion | flops 37765120 | bytes 770048 | tf_op jit(solution)/shard_map/dot_general | solution.py:11
  30.4 0.0 all-gather.2.cloned.1.call-update
  30.4 0.0 copy-done.4
  30.5 0.1 mul.68
  30.6 0.1 add_add_fusion
  30.6 0.1 add.70
  30.7 0.0 copy-done.2
  30.7 0.2 convert_reduce_fusion
  30.9 0.2 select_reduce_fusion
  31.1 0.7 sub.7
  31.8 6.8 %all-to-all-start = ((s32[16,1,20]{2,1,0:T(1,128)}), s32[16,1,20]{2,1,0:T(1,128)S(1)}, u32[]{:S(2)}, u32[]{:S(2)}) async-start(s32[16,1,20]{2,1,0:T(1,128)} %sub.7), calls=%async_computation | async-start | bytes 16384 | tf_op jit(solution)/shard_map/all_to_all | solution.py:59
  38.6 0.0 copy-done.3
  38.6 1.5 %convolution_convert_fusion.2 = bf16[320,1024]{1,0:T(8,128)(2,1)S(1)} fusion(bf16[256,1024]{1,0:T(8,128)(2,1)} %param.19, f32[256]{0:T(256)S(1)} %bitcast.39, s32[256]{0:T(256)S(1)} %multiply_add_fusion), kind=kOutput, calls=%fused_computation.15 | convolution fusion | flops 168968192 | bytes 1181696 | tf_op jit(solution)/shard_map/dot_general | solution.py:11
  40.1 1.0 reshape.90
  41.1 2.2 %all-to-all-done = s32[16,1,20]{2,1,0:T(1,128)S(1)} async-done(((s32[16,1,20]{2,1,0:T(1,128)}), s32[16,1,20]{2,1,0:T(1,128)S(1)}, u32[]{:S(2)}, u32[]{:S(2)}) %all-to-all-start) | async-done | bytes 1312 | tf_op jit(solution)/shard_map/all_to_all | solution.py:59
  43.3 5.8 %all-to-all-start.3 = ((bf16[16,20,1024]{2,1,0:T(8,128)(2,1)}), bf16[16,20,1024]{2,1,0:T(8,128)(2,1)}, u32[]{:S(2)}, u32[]{:S(2)}) async-start(bf16[16,20,1024]{2,1,0:T(8,128)(2,1)} %reshape.90), calls=%async_computation.3 | async-start | bytes 1572864 | tf_op jit(solution)/shard_map/all_to_all | solution.py:57
  49.2 0.6 broadcast.58
  49.7 0.7 reduce.7
  50.5 0.1 eq.47
  50.5 38.2 %all-gather.2.cloned.1.call-done = bf16[256,2048]{0,1:T(8,128)(2,1)} async-done(((bf16[256,64]{0,1:T(8,128)(2,1)}), bf16[256,2048]{0,1:T(8,128)(2,1)}) %all-gather.2.cloned.1.call-update) | async-done | bytes 1048592 | tf_op jit(solution)/shard_map/all_gather | solution.py:36
  88.7 1.5 %fusion.7 = f32[256]{0:T(256)S(1)} fusion(bf16[256,2048]{0,1:T(8,128)(2,1)} %all-gather.2.cloned.1.call-done), kind=kLoop, calls=%fused_computation.11 | loop fusion | flops 1572608 | bytes 1049600 | tf_op jit(solution)/shard_map/reduce_sum | solution.py:38
  90.3 0.0 copy-start.1
  90.3 0.0 copy-start.5
  90.3 0.0 copy-start.6
  90.3 3.3 %fusion.5 = f32[256,704]{0,1:T(8,128)S(1)} fusion(bf16[1,2048,704]{1,2,0:T(8,128)(2,1)} %param.16, bf16[256,2048]{0,1:T(8,128)(2,1)} %all-gather.2.cloned.1.call-done, f32[2048]{0:T(1024)} %param.15, f32[256]{0:T(256)S(1)} %add_rsqrt_fusion), kind=kOutput, calls=%fused_computation.6 | convolution fusion | flops 740294656 | bytes 4662272 | tf_op jit(solution)/shard_map/dot_general | solution.py:11
  93.6 0.0 copy-done.1
  93.6 0.0 copy-done.5
  93.6 0.0 copy-done.6
  93.7 1.0 fusion.17
  94.7 10.6 %all_gather.11 = bf16[256,1408]{0,1:T(8,128)(2,1)} all-gather(bf16[256,704]{0,1:T(8,128)(2,1)S(1)} %fusion.17), channel_id=1, replica_groups=mesh['dp'=2,'expert'=16] {'dp'}, dimensions={1}, use_global_device_ids=true | all-gather | bytes 1081344 | tf_op jit(solution)/shard_map/all_gather | solution.py:66
  105.3 0.0 copy-done
  105.3 2.3 %convolution_convert_fusion.3 = bf16[320,1024]{1,0:T(8,128)(2,1)S(1)} fusion(bf16[256,1408]{0,1:T(8,128)(2,1)} %all_gather.11, bf16[1,1408,1024]{2,1,0:T(8,128)(2,1)S(1)} %copy-done, s32[320]{0:T(512)S(1)} %eq.47), kind=kOutput, calls=%fused_computation.16 | convolution fusion | flops 906641408 | bytes 4261120 | tf_op jit(solution)/shard_map/dot_general | solution.py:11
  107.6 1.0 reshape.88
  108.7 0.0 all-to-all-done.3
  108.7 6.3 %all-to-all-start.2 = ((bf16[16,20,1024]{2,1,0:T(8,128)(2,1)}), bf16[16,20,1024]{2,1,0:T(8,128)(2,1)}, u32[]{:S(2)}, u32[]{:S(2)}) async-start(bf16[16,20,1024]{2,1,0:T(8,128)(2,1)} %reshape.88), calls=%async_computation.2 | async-start | bytes 1572864 | tf_op jit(solution)/shard_map/all_to_all | solution.py:71
  114.9 1.2 reshape.91
  116.2 4.7 %fusion = bf16[1,1408,1024]{2,1,0:T(8,128)(2,1)} fusion(bf16[320,1024]{1,0:T(8,128)(2,1)S(1)} %reshape.91, bf16[256,1408]{0,1:T(8,128)(2,1)} %all_gather.11, s32[320]{0:T(512)S(1)} %eq.47), kind=kOutput, calls=%fused_computation.1 | convolution fusion | flops 1155407872 | bytes 4261120 | tf_op jit(solution)/shard_map/dot_general | solution.py:11
  120.8 13.7 %all-to-all-done.2 = bf16[16,20,1024]{2,1,0:T(8,128)(2,1)} async-done(((bf16[16,20,1024]{2,1,0:T(8,128)(2,1)}), bf16[16,20,1024]{2,1,0:T(8,128)(2,1)}, u32[]{:S(2)}, u32[]{:S(2)}) %all-to-all-start.2) | async-done | bytes 655392 | tf_op jit(solution)/shard_map/all_to_all | solution.py:71
  134.6 1.2 reshape.89
  135.8 1.3 fusion.13
  (4 shorter events, 0.0 us)
Async XLA Ops:
  7.2 98.1 %copy-start = (bf16[1,1408,1024]{2,1,0:T(8,128)(2,1)S(1)}, bf16[1,1408,1024]{2,1,0:T(8,128)(2,1)}, u32[]{:S(2)}) copy-start(bf16[1,1408,1024]{2,1,0:T(8,128)(2,1)} %param.18) | copy-start | bytes 8650756
  7.2 23.3 %copy-start.4 = (s32[2,1,2]{2,1,0:T(1,128)S(1)}, s32[2,1,2]{2,1,0:T(1,128)}, u32[]{:S(2)}) copy-start(s32[2,1,2]{2,1,0:T(1,128)} %param.11) | copy-start | bytes 52
  7.2 23.5 %copy-start.2 = (s32[256,1]{0,1:T(1,128)S(1)}, s32[256,1]{0,1:T(1,128)}, u32[]{:S(2)}) copy-start(s32[256,1]{0,1:T(1,128)} %param.12) | copy-start | bytes 3076
  7.2 31.4 %copy-start.3 = (f32[256,1]{0,1:T(1,128)S(1)}, f32[256,1]{0,1:T(1,128)}, u32[]{:S(2)}) copy-start(f32[256,1]{0,1:T(1,128)} %param.13) | copy-start | bytes 3076
  9.1 15.8 %all-to-all-start.1 = ((bf16[72,16,64]{0,2,1:T(8,128)(2,1)}), bf16[72,16,64]{0,2,1:T(8,128)(2,1)}, u32[]{:S(2)}, u32[]{:S(2)}) async-start(bf16[72,16,64]{0,2,1:T(8,128)(2,1)} %bitcast.3), calls=%async_computation.1 | async-start | bytes 524288 | tf_op jit(solution)/shard_map/all_to_all | solution.py:32
  15.7 73.1 %all-gather.2.cloned.1.call-start = ((), (), s32[]{:S(2)}) async-start(), calls=%async_computation.4 | async-start | bytes 1081344 | tf_op jit(solution)/shard_map/all_gather | solution.py:36
  31.8 11.5 %all-to-all-start = ((s32[16,1,20]{2,1,0:T(1,128)}), s32[16,1,20]{2,1,0:T(1,128)S(1)}, u32[]{:S(2)}, u32[]{:S(2)}) async-start(s32[16,1,20]{2,1,0:T(1,128)} %sub.7), calls=%async_computation | async-start | bytes 16384 | tf_op jit(solution)/shard_map/all_to_all | solution.py:59
  43.3 65.3 %all-to-all-start.3 = ((bf16[16,20,1024]{2,1,0:T(8,128)(2,1)}), bf16[16,20,1024]{2,1,0:T(8,128)(2,1)}, u32[]{:S(2)}, u32[]{:S(2)}) async-start(bf16[16,20,1024]{2,1,0:T(8,128)(2,1)} %reshape.90), calls=%async_computation.3 | async-start | bytes 1572864 | tf_op jit(solution)/shard_map/all_to_all | solution.py:57
  90.3 3.3 %copy-start.1 = (bf16[256,2048]{0,1:T(8,128)(2,1)S(1)}, bf16[256,2048]{0,1:T(8,128)(2,1)}, u32[]{:S(2)}) copy-start(bf16[256,2048]{0,1:T(8,128)(2,1)} %all-gather.2.cloned.1.call-done) | copy-start | bytes 3145732
  90.3 3.3 %copy-start.5 = (bf16[1,2048,704]{1,2,0:T(8,128)(2,1)S(1)}, bf16[1,2048,704]{1,2,0:T(8,128)(2,1)}, u32[]{:S(2)}) copy-start(bf16[1,2048,704]{1,2,0:T(8,128)(2,1)} %param.17) | copy-start | bytes 8650756
  90.3 3.3 %copy-start.6 = (f32[2048]{0:T(1024)S(1)}, f32[2048]{0:T(1024)}, u32[]{:S(2)}) copy-start(f32[2048]{0:T(1024)} %param.15) | copy-start | bytes 24580
  108.7 25.9 %all-to-all-start.2 = ((bf16[16,20,1024]{2,1,0:T(8,128)(2,1)}), bf16[16,20,1024]{2,1,0:T(8,128)(2,1)}, u32[]{:S(2)}, u32[]{:S(2)}) async-start(bf16[16,20,1024]{2,1,0:T(8,128)(2,1)} %reshape.88), calls=%async_computation.2 | async-start | bytes 1572864 | tf_op jit(solution)/shard_map/all_to_all | solution.py:71
Sparse Core Ops, SparseCore 0:
  30.6 58.1 all-gather.1
where the time goes:
time: 145 us; the launch traced here: 144 us
  waiting for transfers between devices  54.2 us (37%)
  starting transfers between devices  25.6 us (18%)
  blocking collectives  19.7 us (14%)
  matrix products  16 us (11%)
  between operations  14.2 us (10%)
  local copies, waits for them, and re-layouts  11.7 us (8%)
  other arithmetic  2.68 us (2%)
    all_gather x1, waiting for transfers between devices, body(): projected = lax.all_gather(part, ('dp', 'expert'), axis=1, tiled=True)  38.2 us
    dot_general x7, matrix products, dot(): return lax.dot_general(a, b, (dims, ((), ())), preferred_element_type=F32)  16 us
    all_to_all x1, waiting for transfers between devices, body(): lax.all_to_all(sent_out, 'expert', split_axis=0, concat_axis=0, tiled=True)  13.7 us
    all_gather x1, blocking collectives, body(): hidden = lax.all_gather(half, 'dp', axis=1, tiled=True)  10.6 us
    all_gather x1, blocking collectives, body(): feats = lax.all_gather(cache, 'dp', axis=0, tiled=True).reshape(-1, feat)  9.12 us
    all_to_all x1, starting transfers between devices, body(): lax.all_to_all(slot_row.reshape(experts, capacity), 'expert', split_axis=...  6.85 us
    all_to_all x1, starting transfers between devices, body(): lax.all_to_all(proj_weight.reshape(-1, n_expert, lanes), 'expert', split_...  6.58 us
    all_to_all x1, starting transfers between devices, body(): lax.all_to_all(sent_out, 'expert', split_axis=0, concat_axis=0, tiled=True)  6.26 us
  transfers between devices with their start and end apart: 5, of which 3 were waited for; matrix products, arithmetic and copies ran while one was open for 14% of the time, Pallas kernels for 0%

commit v1 on v0

--- a/solution.py
+++ b/solution.py
@@ -29,8 +29,16 @@
     block, feat = cache.shape[1:]
     feats = lax.all_gather(cache, "dp", axis=0, tiled=True).reshape(-1, feat)
     lanes = width // n_expert
-    piece = lax.all_to_all(
-        proj_weight.reshape(-1, n_expert, lanes), "expert", split_axis=1, concat_axis=0, tiled=True
+    piece = jnp.concatenate(
+        lax.all_to_all(
+            jnp.stack(
+                jnp.split(proj_weight.reshape(-1, n_expert, lanes), lax.axis_size("expert"), axis=1)
+            ),
+            "expert",
+            0,
+            0,
+        ),
+        axis=0,
     ).reshape(feat, lanes)
     part = dot(feats, piece).astype(BF)
     projected = lax.all_gather(part, ("dp", "expert"), axis=1, tiled=True)

time: 145 us -> 162 us (1.12)
  local copies, waits for them, and re-layouts: 11.7 us -> 28.1 us
    unnamed x14 -> x29, local copies, waits for them, and re-layouts: 0.04 us -> 9.17 us
    split x0 -> x17, local copies, waits for them, and re-layouts: none -> 7.31 us  [body(): jnp.split(proj_weight.reshape(-1, n_expert, lanes), lax.axis_size('expert...]
    another operation x0 -> x2, local copies, waits for them, and re-layouts: none -> 2.5 us  [the longest x1 1.89 us: body(): piece = jnp.concatenate(lax.all_to_all(jnp.stack(jnp.split(proj_weight.re...]
    reshape x1 -> x0, local copies, waits for them, and re-layouts: 1.89 us -> none  [body(): piece = lax.all_to_all(proj_weight.reshape(-1, n_expert, lanes), 'expert'...]
  transfers between devices with their start and end apart: 5 -> 5, of which waited for: 3 -> 3; matrix products, arithmetic and copies ran while one was open for 14% -> 13% of each run, Pallas kernels for 0% -> 0%
where the time goes in v1:
time: 162 us; the launch traced here: 161 us
  waiting for transfers between devices  54.4 us (34%)
  local copies, waits for them, and re-layouts  28.1 us (17%)
  starting transfers between devices  25.6 us (16%)
  blocking collectives  19.7 us (12%)
  matrix products  16 us (10%)
  between operations  14.3 us (9%)
  other arithmetic  2.54 us (2%)
    all_gather x1, waiting for transfers between devices, body(): projected = lax.all_gather(part, ('dp', 'expert'), axis=1, tiled=True)  38.5 us
    dot_general x7, matrix products, dot(): return lax.dot_general(a, b, (dims, ((), ())), preferred_element_type=F32)  16 us
    all_to_all x1, waiting for transfers between devices, body(): lax.all_to_all(sent_out, 'expert', split_axis=0, concat_axis=0, tiled=True)  13.7 us
    all_gather x1, blocking collectives, body(): hidden = lax.all_gather(half, 'dp', axis=1, tiled=True)  10.6 us
    unnamed x29, local copies, waits for them, and re-layouts  9.17 us
    all_gather x1, blocking collectives, body(): feats = lax.all_gather(cache, 'dp', axis=0, tiled=True).reshape(-1, feat)  9.12 us
    split x17, local copies, waits for them, and re-layouts, body(): jnp.split(proj_weight.reshape(-1, n_expert, lanes), lax.axis_size('expert...  7.31 us
    all_to_all x1, starting transfers between devices, body(): lax.all_to_all(slot_row.reshape(experts, capacity), 'expert', split_axis=...  6.85 us
  transfers between devices with their start and end apart: 5, of which 3 were waited for; matrix products, arithmetic and copies ran while one was open for 13% of the time, Pallas kernels for 0%

profile of v1, /device:TPU:9, one launch (start us, length us, event | category | flops | bytes accessed | tf_op | source)
XLA Modules:
  0.0 160.5 jit_solution(14853586819270656399)
XLA Ops:
  7.2 1.3 reshape.81
  8.5 1.1 fusion.32
  9.7 0.9 copy.422
  10.5 0.6 constant_dynamic-update-slice_fusion.15
  11.1 0.9 copy.423
  12.0 0.9 copy.424
  12.9 0.9 copy.425
  13.7 0.9 copy.426
  14.6 0.9 copy.427
  15.5 0.1 copy.428
  15.6 0.1 copy.429
  15.7 0.1 copy.430
  15.8 0.1 copy.431
  15.9 0.1 copy.432
  16.0 0.1 copy.433
  16.1 0.1 copy.434
  16.2 0.1 copy.435
  16.3 0.1 copy.436
  16.4 0.1 copy.437
  16.5 0.6 constant_dynamic-update-slice_fusion.14
  17.1 0.6 constant_dynamic-update-slice_fusion.13
  17.7 0.6 constant_dynamic-update-slice_fusion.12
  18.4 0.6 constant_dynamic-update-slice_fusion.11
  19.0 0.6 constant_dynamic-update-slice_fusion.10
  19.6 0.6 constant_dynamic-update-slice_fusion.9
  20.2 0.6 constant_dynamic-update-slice_fusion.8
  20.8 0.6 constant_dynamic-update-slice_fusion.7
  21.4 0.6 constant_dynamic-update-slice_fusion.6
  22.0 0.6 constant_dynamic-update-slice_fusion.5
  22.6 0.6 constant_dynamic-update-slice_fusion.4
  23.2 0.6 constant_dynamic-update-slice_fusion.3
  23.8 0.6 constant_dynamic-update-slice_fusion.2
  24.4 0.6 constant_dynamic-update-slice_fusion.1
  25.0 0.6 constant_dynamic-update-slice_fusion
  25.6 6.6 %all-to-all-start.1 = ((bf16[16,72,1,64]{1,3,2,0:T(8,128)(2,1)}), bf16[16,72,1,64]{1,3,2,0:T(8,128)(2,1)}, u32[]{:S(2)}, u32[]{:S(2)}) async-start(bf16[16,72,1,64]{1,3,2,0:T(8,128)(2,1)} %constant_dynamic-update-slice_fusion), calls=%async_computation.1 | async-start | bytes 524288 | tf_op jit(solution)/shard_map/all_to_all | solution.py:33
  32.3 9.1 %all_gather.9 = bf16[4,64,1152]{2,1,0:T(8,128)(2,1)S(1)} all-gather(bf16[2,64,1152]{2,1,0:T(8,128)(2,1)} %param.10), channel_id=1, replica_groups=mesh['dp'=2,'expert'=16] {'dp'}, dimensions={0}, use_global_device_ids=true | all-gather | bytes 884736 | tf_op jit(solution)/shard_map/all_gather | solution.py:30
  41.4 1.8 %copy.438 = bf16[16,72,1,64]{1,0,3,2:T(8,128)(2,1)} copy(bf16[16,72,1,64]{1,3,2,0:T(8,128)(2,1)} %all-to-all-done.1) | data formatting | bytes 294912 | tf_op jit(solution)/shard_map/all_to_all | solution.py:33
  43.2 1.9 %reshape_reshape.3 = bf16[1152,64]{0,1:T(8,128)(2,1)} reshape(bf16[16,72,1,64]{1,0,3,2:T(8,128)(2,1)} %copy.438) | data formatting | bytes 294912 | tf_op jit(solution)/shard_map/reshape;reshape | solution.py:42
  45.1 1.8 %fusion.22 = bf16[256,64]{0,1:T(8,128)(2,1)} fusion(bf16[1152,64]{0,1:T(8,128)(2,1)} %reshape_reshape.3, bf16[256,1152]{1,0:T(8,128)(2,1)S(1)} %bitcast.66), kind=kOutput, calls=%fused_computation.22 | convolution fusion | flops 37765120 | bytes 770048 | tf_op jit(solution)/shard_map/dot_general | solution.py:11
  47.0 0.1 mul.68
  47.2 0.2 convert_reduce_fusion
  47.4 0.2 select_reduce_fusion
  47.6 0.7 sub.7
  48.3 6.8 %all-to-all-start = ((s32[16,1,20]{2,1,0:T(1,128)}), s32[16,1,20]{2,1,0:T(1,128)S(1)}, u32[]{:S(2)}, u32[]{:S(2)}) async-start(s32[16,1,20]{2,1,0:T(1,128)} %sub.7), calls=%async_computation | async-start | bytes 16384 | tf_op jit(solution)/shard_map/all_to_all | solution.py:67
  55.1 1.5 convolution_convert_fusion.2
  56.6 1.0 reshape.85
  57.6 2.2 %all-to-all-done = s32[16,1,20]{2,1,0:T(1,128)S(1)} async-done(((s32[16,1,20]{2,1,0:T(1,128)}), s32[16,1,20]{2,1,0:T(1,128)S(1)}, u32[]{:S(2)}, u32[]{:S(2)}) %all-to-all-start) | async-done | bytes 1312 | tf_op jit(solution)/shard_map/all_to_all | solution.py:67
  59.8 5.8 %all-to-all-start.3 = ((bf16[16,20,1024]{2,1,0:T(8,128)(2,1)}), bf16[16,20,1024]{2,1,0:T(8,128)(2,1)}, u32[]{:S(2)}, u32[]{:S(2)}) async-start(bf16[16,20,1024]{2,1,0:T(8,128)(2,1)} %reshape.85), calls=%async_computation.3 | async-start | bytes 1572864 | tf_op jit(solution)/shard_map/all_to_all | solution.py:65
  65.7 0.5 broadcast.58
  66.2 0.6 reduce.7
  66.7 0.1 eq.47
  66.8 38.5 %all-gather.2.cloned.1.call-done = bf16[256,2048]{0,1:T(8,128)(2,1)} async-done(((bf16[256,64]{0,1:T(8,128)(2,1)}), bf16[256,2048]{0,1:T(8,128)(2,1)}) %all-gather.2.cloned.1.call-update) | async-done | bytes 1048592 | tf_op jit(solution)/shard_map/all_gather | solution.py:44
  105.3 1.5 fusion.7
  106.8 3.3 %fusion.5 = f32[256,704]{0,1:T(8,128)S(1)} fusion(bf16[1,2048,704]{1,2,0:T(8,128)(2,1)} %param.16, bf16[256,2048]{0,1:T(8,128)(2,1)} %all-gather.2.cloned.1.call-done, f32[2048]{0:T(1024)} %param.15, f32[256]{0:T(256)S(1)} %add_rsqrt_fusion), kind=kOutput, calls=%fused_computation.6 | convolution fusion | flops 740294656 | bytes 4662272 | tf_op jit(solution)/shard_map/dot_general | solution.py:11
  110.2 1.0 fusion.17
  111.2 10.6 %all_gather.11 = bf16[256,1408]{0,1:T(8,128)(2,1)} all-gather(bf16[256,704]{0,1:T(8,128)(2,1)S(1)} %fusion.17), channel_id=1, replica_groups=mesh['dp'=2,'expert'=16] {'dp'}, dimensions={1}, use_global_device_ids=true | all-gather | bytes 1081344 | tf_op jit(solution)/shard_map/all_gather | solution.py:74
  121.8 2.3 %convolution_convert_fusion.3 = bf16[320,1024]{1,0:T(8,128)(2,1)S(1)} fusion(bf16[256,1408]{0,1:T(8,128)(2,1)} %all_gather.11, bf16[1,1408,1024]{2,1,0:T(8,128)(2,1)S(1)} %copy-done, s32[320]{0:T(512)S(1)} %eq.47), kind=kOutput, calls=%fused_computation.16 | convolution fusion | flops 906641408 | bytes 4261120 | tf_op jit(solution)/shard_map/dot_general | solution.py:11
  124.1 1.0 reshape.83
  125.2 6.3 %all-to-all-start.2 = ((bf16[16,20,1024]{2,1,0:T(8,128)(2,1)}), bf16[16,20,1024]{2,1,0:T(8,128)(2,1)}, u32[]{:S(2)}, u32[]{:S(2)}) async-start(bf16[16,20,1024]{2,1,0:T(8,128)(2,1)} %reshape.83), calls=%async_computation.2 | async-start | bytes 1572864 | tf_op jit(solution)/shard_map/all_to_all | solution.py:79
  131.5 1.2 reshape.86
  132.7 4.7 %fusion = bf16[1,1408,1024]{2,1,0:T(8,128)(2,1)} fusion(bf16[320,1024]{1,0:T(8,128)(2,1)S(1)} %reshape.86, bf16[256,1408]{0,1:T(8,128)(2,1)} %all_gather.11, s32[320]{0:T(512)S(1)} %eq.47), kind=kOutput, calls=%fused_computation.1 | convolution fusion | flops 1155407872 | bytes 4261120 | tf_op jit(solution)/shard_map/dot_general | solution.py:11
  137.4 13.7 %all-to-all-done.2 = bf16[16,20,1024]{2,1,0:T(8,128)(2,1)} async-done(((bf16[16,20,1024]{2,1,0:T(8,128)(2,1)}), bf16[16,20,1024]{2,1,0:T(8,128)(2,1)}, u32[]{:S(2)}, u32[]{:S(2)}) %all-to-all-start.2) | async-done | bytes 655392 | tf_op jit(solution)/shard_map/all_to_all | solution.py:79
  151.1 1.2 reshape.84
  152.4 1.3 fusion.13
  (24 shorter events, 0.3 us)
Async XLA Ops:
  7.2 114.6 %copy-start = (bf16[1,1408,1024]{2,1,0:T(8,128)(2,1)S(1)}, bf16[1,1408,1024]{2,1,0:T(8,128)(2,1)}, u32[]{:S(2)}) copy-start(bf16[1,1408,1024]{2,1,0:T(8,128)(2,1)} %param.18) | copy-start | bytes 8650756
  8.5 38.5 %copy-start.4 = (s32[2,1,2]{2,1,0:T(1,128)S(1)}, s32[2,1,2]{2,1,0:T(1,128)}, u32[]{:S(2)}) copy-start(s32[2,1,2]{2,1,0:T(1,128)} %param.11) | copy-start | bytes 52
  8.5 38.8 %copy-start.2 = (s32[256,1]{0,1:T(1,128)S(1)}, s32[256,1]{0,1:T(1,128)}, u32[]{:S(2)}) copy-start(s32[256,1]{0,1:T(1,128)} %param.12) | copy-start | bytes 3076
  25.6 15.8 %all-to-all-start.1 = ((bf16[16,72,1,64]{1,3,2,0:T(8,128)(2,1)}), bf16[16,72,1,64]{1,3,2,0:T(8,128)(2,1)}, u32[]{:S(2)}, u32[]{:S(2)}) async-start(bf16[16,72,1,64]{1,3,2,0:T(8,128)(2,1)} %constant_dynamic-update-slice_fusion), calls=%async_computation.1 | async-start | bytes 524288 | tf_op jit(solution)/shard_map/all_to_all | solution.py:33
  32.2 73.1 %all-gather.2.cloned.1.call-start = ((), (), s32[]{:S(2)}) async-start(), calls=%async_computation.4 | async-start | bytes 1081344 | tf_op jit(solution)/shard_map/all_gather | solution.py:44
  48.3 11.5 %all-to-all-start = ((s32[16,1,20]{2,1,0:T(1,128)}), s32[16,1,20]{2,1,0:T(1,128)S(1)}, u32[]{:S(2)}, u32[]{:S(2)}) async-start(s32[16,1,20]{2,1,0:T(1,128)} %sub.7), calls=%async_computation | async-start | bytes 16384 | tf_op jit(solution)/shard_map/all_to_all | solution.py:67
  59.8 65.3 %all-to-all-start.3 = ((bf16[16,20,1024]{2,1,0:T(8,128)(2,1)}), bf16[16,20,1024]{2,1,0:T(8,128)(2,1)}, u32[]{:S(2)}, u32[]{:S(2)}) async-start(bf16[16,20,1024]{2,1,0:T(8,128)(2,1)} %reshape.85), calls=%async_computation.3 | async-start | bytes 1572864 | tf_op jit(solution)/shard_map/all_to_all | solution.py:65
  106.8 3.3 %copy-start.1 = (bf16[256,2048]{0,1:T(8,128)(2,1)S(1)}, bf16[256,2048]{0,1:T(8,128)(2,1)}, u32[]{:S(2)}) copy-start(bf16[256,2048]{0,1:T(8,128)(2,1)} %all-gather.2.cloned.1.call-done) | copy-start | bytes 3145732
  106.8 3.3 %copy-start.5 = (bf16[1,2048,704]{1,2,0:T(8,128)(2,1)S(1)}, bf16[1,2048,704]{1,2,0:T(8,128)(2,1)}, u32[]{:S(2)}) copy-start(bf16[1,2048,704]{1,2,0:T(8,128)(2,1)} %param.17) | copy-start | bytes 8650756
  106.8 3.3 %copy-start.6 = (f32[2048]{0:T(1024)S(1)}, f32[2048]{0:T(1024)}, u32[]{:S(2)}) copy-start(f32[2048]{0:T(1024)} %param.15) | copy-start | bytes 24580
  125.2 25.9 %all-to-all-start.2 = ((bf16[16,20,1024]{2,1,0:T(8,128)(2,1)}), bf16[16,20,1024]{2,1,0:T(8,128)(2,1)}, u32[]{:S(2)}, u32[]{:S(2)}) async-start(bf16[16,20,1024]{2,1,0:T(8,128)(2,1)} %reshape.83), calls=%async_computation.2 | async-start | bytes 1572864 | tf_op jit(solution)/shard_map/all_to_all | solution.py:79
  132.7 19.7 %copy-start.3 = (f32[256,1]{0,1:T(1,128)S(1)}, f32[256,1]{0,1:T(1,128)}, u32[]{:S(2)}) copy-start(f32[256,1]{0,1:T(1,128)} %param.13) | copy-start | bytes 3076
Sparse Core Ops, SparseCore 0:
  47.1 58.1 all-gather.1
